TPU v7x, 512 devices: a whole 4x4x16 slice. The times are simulated.
512 devices in a mesh: grp: 64 (over z_hi, y, x), intra: 8 (over z_lo, core).
Axes of the slice: x: 4, y: 4, z: 16 (z_hi: 4, z_lo: 4; z = z_hi * 4 + z_lo), core: 2. Of those that a mesh axis runs over, the one named last changes fastest.
Arguments:
- activations: bfloat16 [20480, 14848], P('grp', 'intra'), may hold values from -400 to 400
- norm_gain: bfloat16 [14848], P(('intra', 'grp')), may hold values from 0.099609375 to 1.8984375
- norm_bias: bfloat16 [14848], P(('intra', 'grp')), may hold values from -3 to 3
- kv_weight: bfloat16 [14848, 512], P(('intra', 'grp')), may hold values from -0.046875 to 0.046875
- kv_cotangent: bfloat16 [20480, 512], P(('grp', 'intra')), may hold values from -6 to 6
Outputs:
- projected: bfloat16 [20480, 512], P(('grp', 'intra'))
- input_grad: bfloat16 [20480, 14848], P('grp', 'intra')
- weight_grad: float32 [14848, 512], P(('intra', 'grp'))
- gain_grad: float32 [14848], P(('intra', 'grp'))
- bias_grad: float32 [14848], P(('intra', 'grp'))
All inputs are finite; a program needn't handle non-finite values.
Results may differ from a plain program's by a relative error of at most 0.017.
Values may be sent and summed in bfloat16 or wider, within the bound.
A program may use at most 64 MiB of HBM per device.

v0:
```python
import jax
import jax.numpy as jnp
from jax import lax
from jax.sharding import PartitionSpec as P

epsilon = 1e-05


def shards(activations, norm_gain, norm_bias, kv_weight, kv_cotangent):
    weight_rows, gain_rows, bias_rows = (
        lax.all_gather(kv_weight, "grp", axis=0, tiled=True),
        lax.all_gather(norm_gain, "grp", axis=0, tiled=True),
        lax.all_gather(norm_bias, "grp", axis=0, tiled=True),
    )
    norm_scale = gain_rows.astype(jnp.float32)
    offset = bias_rows.astype(jnp.float32)
    floats = activations.astype(jnp.float32)
    feature_count = floats.shape[1] * lax.axis_size("intra")
    totals, squares = lax.psum((jnp.sum(floats, axis=1), jnp.sum(floats * floats, axis=1)), "intra")
    average = (totals / feature_count)[:, None]
    spread = (squares / feature_count)[:, None] - average * average
    inverse = lax.rsqrt(spread + epsilon)
    centred = (floats - average) * inverse
    normed = (centred * norm_scale + offset).astype(jnp.bfloat16)
    partial_value = jnp.dot(normed, weight_rows, preferred_element_type=jnp.float32)
    projected = lax.psum_scatter(
        partial_value.astype(jnp.bfloat16), "intra", scatter_dimension=0, tiled=True
    )
    cotangent = lax.all_gather(kv_cotangent, "intra", axis=0, tiled=True)
    normed_grad = lax.dot_general(
        cotangent, weight_rows, (((1,), (1,)), ((), ())), preferred_element_type=jnp.float32
    )
    scaled = normed_grad * norm_scale
    grad_sum, cross_sum = lax.psum(
        (jnp.sum(scaled, axis=1), jnp.sum(scaled * centred, axis=1)), "intra"
    )
    grad_mean = (grad_sum / feature_count)[:, None]
    cross_mean = (cross_sum / feature_count)[:, None]
    input_grad = (inverse * (scaled - grad_mean - centred * cross_mean)).astype(jnp.bfloat16)
    gain_part = jnp.sum(normed_grad * centred, axis=0)
    bias_part = jnp.sum(normed_grad, axis=0)
    local_grad = lax.dot_general(
        normed, cotangent, (((0,), (0,)), ((), ())), preferred_element_type=jnp.float32
    )
    weight_grad, gain_grad, bias_grad = (
        lax.psum_scatter(local_grad, "grp", scatter_dimension=0, tiled=True),
        lax.psum_scatter(gain_part, "grp", scatter_dimension=0, tiled=True),
        lax.psum_scatter(bias_part, "grp", scatter_dimension=0, tiled=True),
    )
    return (projected, input_grad, weight_grad, gain_grad, bias_grad)


def solution(mesh):
    return jax.shard_map(
        shards,
        mesh=mesh,
        in_specs=(
            P("grp", "intra"),
            P(("intra", "grp")),
            P(("intra", "grp")),
            P(("intra", "grp"), None),
            P(("grp", "intra"), None),
        ),
        out_specs=(
            P(("grp", "intra"), None),
            P("grp", "intra"),
            P(("intra", "grp"), None),
            P(("intra", "grp")),
            P(("intra", "grp")),
        ),
        check_vma=False,
    )
```

profile of v0, /device:TPU:320, one launch (start us, length us, event | category | flops | bytes accessed | tf_op | source)
XLA Modules:
  0.0 1064.6 jit_solution(1258641226300417632)
XLA Ops:
  8.0 1.4 fusion.17
  10.0 0.9 dynamic-update-slice.1
  10.9 0.8 dynamic-update-slice
  11.7 226.4 %all-reduce.9 = (bf16[1856]{0:T(1024)(128)(2,1)S(1)}, bf16[1856]{0:T(1024)(128)(2,1)S(1)}) all-reduce(bf16[1856]{0:T(1024)(128)(2,1)S(1)} %dynamic-update-slice.1, bf16[1856]{0:T(1024)(128)(2,1)S(1)} %dynamic-update-slice), channel_id=1, replica_groups=mesh['grp'=64,'intra'=8] {'grp'}, use_global_device_ids=true, to_apply=%add.1 | all-reduce | flops 3712 | bytes 14848
  238.1 1.7 convert_reduce_fusion
  239.8 15.8 %all_gather.15 = bf16[320,512]{1,0:T(8,128)(2,1)S(1)} all-gather(bf16[40,512]{1,0:T(8,128)(2,1)} %param.9), channel_id=1, replica_groups=mesh['grp'=64,'intra'=8] {'intra'}, dimensions={0}, use_global_device_ids=true | all-gather | bytes 368640 | tf_op jit(solution)/shard_map/all_gather | solution.py:29
  255.6 12.4 %all-reduce.8 = (f32[320]{0:T(512)S(1)}, f32[320]{0:T(512)S(1)}) all-reduce(f32[320]{0:T(512)S(1)} %get-tuple-element.10, f32[320]{0:T(512)S(1)} %get-tuple-element.9), channel_id=1, replica_groups=mesh['grp'=64,'intra'=8] {'intra'}, use_global_device_ids=true, to_apply=%region_3.0 | all-reduce | flops 640 | bytes 5120 | tf_op jit(solution)/shard_map/psum | solution.py:19
  268.0 4.4 fusion.14
  272.5 283.4 %fusion = f32[32,512]{1,0:T(8,128)S(1)} fusion(f32[1856,512]{1,0:T(8,128)} %fusion.14), kind=kCustom, calls=%all-reduce-scatter | all-reduce-scatter fusion | flops 1048577 | bytes 3868672
  555.9 1.9 collective-permute-start.5
  557.8 1.9 collective-permute-start.4
  559.8 17.9 %collective-permute-start.3 = (f32[32,512]{1,0:T(8,128)S(1)}, f32[32,512]{1,0:T(8,128)S(1)}, u32[]{:S(2)}, u32[]{:S(2)}) collective-permute-start(f32[32,512]{1,0:T(8,128)S(1)} %fusion), channel_id=1, source_target_pairs={{0,32},{8,40},{16,48},{24,56},{32,64},{40,72},{48,80},{56,88},{64,... | collective-permute-start | bytes 196616
  577.6 5.0 collective-permute-start.2
  582.6 9.7 collective-permute-start.1
  592.4 1.9 collective-permute-start
  595.7 6.4 collective-permute-done.1
  602.1 4.6 collective-permute-done
  606.7 0.9 concatenate
  608.2 2.6 reshape.27
  610.8 1.6 convolution_convert_fusion
  612.4 2.6 fusion.12
  615.0 10.0 all-reduce.7
  625.0 428.0 %all-reduce.6 = (f32[1856]{0:T(1024)S(1)}, f32[1856]{0:T(1024)S(1)}) all-reduce(f32[1856]{0:T(1024)S(1)} %get-tuple-element.5, f32[1856]{0:T(1024)S(1)} %get-tuple-element.8), channel_id=4, replica_groups=mesh['grp'=64,'intra'=8] {'grp'}, use_global_device_ids=true, to_apply=%region_11.0.clone | all-reduce | flops 3712 | bytes 29696
  1054.2 3.5 fusion.11
  (22 shorter events, 2.6 us)
Async XLA Ops:
  7.2 601.0 %all-gather.3.cloned.1.call-start = ((), (), s32[]{:S(2)}) async-start(), calls=%async_computation.2 | async-start | bytes 2129920 | tf_op jit(solution)/shard_map/all_gather | solution.py:11
  7.9 1049.9 %reduce-scatter.4.cloned.1.call-start = ((), (), s32[]{:S(2)}) async-start(), calls=%async_computation.1 | async-start | bytes 368640 | tf_op jit(solution)/shard_map/reduce_scatter | solution.py:26
  555.9 36.5 %collective-permute-start.5 = (f32[29,512]{1,0:T(8,128)S(1)}, f32[29,512]{1,0:T(8,128)S(1)}, u32[]{:S(2)}, u32[]{:S(2)}) collective-permute-start(f32[29,512]{1,0:T(8,128)S(1)} %slice), channel_id=1, source_target_pairs={{0,48},{8,56},{16,64},{24,72},{32,80},{40,88},{48,96},{56,104},{64... | collective-permute-start | bytes 178184
  557.8 37.8 %collective-permute-start.4 = (f32[32,512]{1,0:T(8,128)S(1)}, f32[32,512]{1,0:T(8,128)S(1)}, u32[]{:S(2)}, u32[]{:S(2)}) collective-permute-start(f32[32,512]{1,0:T(8,128)S(1)} %fusion), channel_id=1, source_target_pairs={{0,40},{8,48},{16,56},{24,64},{32,72},{40,80},{48,88},{56,96},{64,... | collective-permute-start | bytes 196616
  559.8 35.9 %collective-permute-start.3 = (f32[32,512]{1,0:T(8,128)S(1)}, f32[32,512]{1,0:T(8,128)S(1)}, u32[]{:S(2)}, u32[]{:S(2)}) collective-permute-start(f32[32,512]{1,0:T(8,128)S(1)} %fusion), channel_id=1, source_target_pairs={{0,32},{8,40},{16,48},{24,56},{32,64},{40,72},{48,80},{56,88},{64,... | collective-permute-start | bytes 196616
  577.6 18.0 %collective-permute-start.2 = (f32[32,512]{1,0:T(8,128)S(1)}, f32[32,512]{1,0:T(8,128)S(1)}, u32[]{:S(2)}, u32[]{:S(2)}) collective-permute-start(f32[32,512]{1,0:T(8,128)S(1)} %fusion), channel_id=1, source_target_pairs={{0,24},{8,32},{16,40},{24,48},{32,56},{40,64},{48,72},{56,80},{64,... | collective-permute-start | bytes 196616
  582.6 19.4 %collective-permute-start.1 = (f32[32,512]{1,0:T(8,128)S(1)}, f32[32,512]{1,0:T(8,128)S(1)}, u32[]{:S(2)}, u32[]{:S(2)}) collective-permute-start(f32[32,512]{1,0:T(8,128)S(1)} %fusion), channel_id=1, source_target_pairs={{0,16},{8,24},{16,32},{24,40},{32,48},{40,56},{48,64},{56,72},{64,... | collective-permute-start | bytes 196616
  592.4 14.3 %collective-permute-start = (f32[32,512]{1,0:T(8,128)S(1)}, f32[32,512]{1,0:T(8,128)S(1)}, u32[]{:S(2)}, u32[]{:S(2)}) collective-permute-start(f32[32,512]{1,0:T(8,128)S(1)} %fusion), channel_id=1, source_target_pairs={{0,8},{8,16},{16,24},{24,32},{32,40},{40,48},{48,56},{56,64},{64,7... | collective-permute-start | bytes 196616
  595.6 15.2 %copy-start = (bf16[320,1856]{1,0:T(8,128)(2,1)S(1)}, bf16[320,1856]{1,0:T(8,128)(2,1)}, u32[]{:S(2)}) copy-start(bf16[320,1856]{1,0:T(8,128)(2,1)} %param.5) | copy-start | bytes 3563524
Sparse Core Ops, SparseCore 0:
  12.2 109.4 all-gather.2
  615.1 28.8 reduce-scatter.3
where the time goes:
time: 1070 us; the launch traced here: 1060 us
  blocking collectives  976 us (91%)
  starting transfers between devices  38.4 us (4%)
  between operations  16.2 us (2%)
  waiting for transfers between devices  11.7 us (1%)
    unnamed x3, blocking collectives  938 us
    unnamed x6, starting transfers between devices  38.4 us
  transfers between devices with their start and end apart: 8, of which 2 were waited for; matrix products, arithmetic and copies ran while one was open for 28% of the time, Pallas kernels for 0%

commit v1 on v0

v1 whole, which is shorter than its diff:
```python
import jax
import jax.numpy as jnp
from jax import lax
from jax.experimental import pallas as pl
from jax.experimental.pallas import tpu as pltpu
from jax.sharding import PartitionSpec as P

epsilon = 1e-05
F32, BF16 = jnp.float32, jnp.bfloat16
MESH = pl.DeviceIdType.MESH

T = 320
F = 1856
C = 512
H = 256
R = 29
SLOT = 32
OWN = 40
NI = 8
D = F * NI
COPIES = 80


def pack(v):
    tail = jnp.concatenate([v[32:40, :H], v[32:40, H:]], axis=0)
    return jnp.concatenate([v[0:16], v[16:32], tail], axis=1)


def unpack(v):
    tail = jnp.concatenate([v[0:8, 1024:], v[8:16, 1024:]], axis=1)
    return jnp.concatenate([v[:, :C], v[:, C:1024], tail], axis=0)


def iota(shape, dim):
    return lax.broadcasted_iota(jnp.int32, shape, dim)


def kernel(
    x_hbm, w_ref, gain_ref, bias_ref, cot_ref,
    proj_ref, ig_hbm, wg_ref, gg_ref, bg_ref,
    xv, cv, igv, wfull, spread_m, squeeze_m, cot32, cotb, cotg, m32, wc, part32,
    gath, scat, land1, land2, scat2, land3, land4, scat3, land5, land6,
    st, stats1, stats2, cols, cols2, pown, pland,
    sends, recvs, local,
):
    grp, me = lax.axis_index("grp"), lax.axis_index("intra")
    z, y, x = grp // 16, (grp // 4) % 4, grp % 4
    core = me % 2

    def up(v, by):
        return (v + by) % 4

    def to_grp(axis, by):
        if axis == "z":
            return {"grp": up(z, by) * 16 + y * 4 + x, "intra": me}
        if axis == "y":
            return {"grp": z * 16 + up(y, by) * 4 + x, "intra": me}
        return {"grp": z * 16 + y * 4 + up(x, by), "intra": me}

    count = [0]

    def remote(src, dst, device):
        k = count[0]
        count[0] += 1
        return pltpu.make_async_remote_copy(
            src_ref=src, dst_ref=dst, send_sem=sends.at[k], recv_sem=recvs.at[k],
            device_id={"grp": device["grp"], "intra": device["intra"]}, device_id_type=MESH,
        )

    started = []

    def start(copies):
        for c in copies:
            c.start()
            started.append(c)
        return copies

    def arrive(copies):
        for c in copies:
            c.wait_recv()

    x_copy = pltpu.make_async_copy(x_hbm, xv, local.at[0])
    x_copy.start()

    peers = [to_grp(a, by) for a in "zyx" for by in (1, 3)]
    peers += [{"grp": grp, "intra": (me + d) % NI} for d in range(1, NI)]
    barrier = pltpu.get_barrier_semaphore()
    for peer in peers:
        pl.semaphore_signal(barrier, inc=1, device_id=peer, device_id_type=MESH)

    diagonal = iota((SLOT, R), 0) == iota((SLOT, R), 1)

    def column(ref):
        row = ref[...].astype(F32)
        return jnp.sum(jnp.where(diagonal, row, 0.0), axis=1, keepdims=True)

    gain, bias = column(gain_ref), column(bias_ref)
    wfull[...] = jnp.zeros_like(wfull)
    wfull[0:R, :] = w_ref[...].astype(F32)
    weight = wfull[...]
    product = jnp.sum(weight * bias, axis=0, keepdims=True)
    high = product.astype(BF16).astype(F32)
    row = iota((SLOT, C), 0)
    slot = jnp.where(row == R, high, jnp.where(row == R + 1, product - high, weight * gain)).astype(BF16)
    gath[0, z, y, x] = slot[:, :H]
    gath[1, z, y, x] = slot[:, H:]
    cotg[me] = pack(cot_ref[...].astype(F32)).astype(BF16)

    pl.semaphore_wait(barrier, len(peers))

    gz1 = start([
        remote(gath.at[:, z, y, x], gath.at[:, z, y, x], to_grp("z", 1)),
        remote(gath.at[:, z, y, x], gath.at[:, z, y, x], to_grp("z", 3)),
    ])
    mate = {"grp": grp, "intra": me + 1 - 2 * core}
    ct1 = start([remote(cotg.at[me], cotg.at[me], mate)])
    ct1 += start([
        remote(cotg.at[me], cotg.at[me], {"grp": grp, "intra": (me + d) % NI}) for d in (2, 6, 4)
    ])

    a, b = iota((H, 8 * R), 0), iota((H, 8 * R), 1)
    spread_m[...] = jnp.where(((a & 31) < R) & (b == R * (a >> 5) + (a & 31)), 1.0, 0.0).astype(BF16)
    a, b = iota((240, H), 0), iota((240, H), 1)
    within = b & 31
    hit = (within < R) & ((a == R * (b >> 5) + within) | (a == 233))
    hit = hit | ((within >= R) & (within < R + 2) & (a == 232))
    squeeze_m[...] = jnp.where(hit, 1.0, 0.0).astype(BF16)

    x_copy.wait()
    st[...] = jnp.zeros_like(st)
    lane = iota((64, 128), 1)
    for r in range(0, T, 64):
        v = xv[r:r + 64, :].astype(F32)
        s1 = jnp.sum(v, axis=1, keepdims=True)
        s2 = jnp.sum(v * v, axis=1, keepdims=True)
        st[r:r + 64, :] = jnp.where(lane == 0, s1, jnp.where(lane == 1, s2, 0.0))
    stats1[me] = st[...].T[0:2, :]
    ex1 = start([
        remote(stats1.at[me], stats1.at[me], {"grp": grp, "intra": (me + d) % NI}) for d in range(1, NI)
    ])

    arrive(gz1)
    gz2 = start([
        remote(gath.at[0, up(z, 3), y, x], gath.at[0, up(z, 3), y, x], to_grp("z", 1)),
        remote(gath.at[1, up(z, 1), y, x], gath.at[1, up(z, 1), y, x], to_grp("z", 3)),
    ])
    arrive(ct1)
    ct2 = start([
        remote(cotg.at[(me + d) % NI], cotg.at[(me + d) % NI], mate) for d in (6, 2, 4)
    ])

    def stage(views, axes):
        first = []
        for h in (0, 1):
            p = {"y": y, "x": x}[axes[h]]
            first += [
                remote(views[h](p, 0), views[h](p, 0), to_grp(axes[h], 1)),
                remote(views[h](p, 0), views[h](p, 0), to_grp(axes[h], 3)),
            ]
        return start(first)

    def forward(views, axes, first):
        second = []
        for h in (0, 1):
            p = {"y": y, "x": x}[axes[h]]
            arrive(first[2 * h:2 * h + 2])
            second += start([
                remote(views[h](up(p, 3), 1), views[h](up(p, 3), 1), to_grp(axes[h], 1)),
                remote(views[h](up(p, 1), 2), views[h](up(p, 1), 2), to_grp(axes[h], 3)),
            ])
        return second

    part_of = (slice(None), slice(0, 2), slice(2, 4))
    g2 = (
        lambda p, part: gath.at[0, part_of[part], p, x],
        lambda p, part: gath.at[1, part_of[part], y, p],
    )
    g3 = (
        lambda p, part: gath.at[0, part_of[part], :, p],
        lambda p, part: gath.at[1, part_of[part], p, :],
    )

    arrive(gz2)
    s2a = stage(g2, "yx")

    arrive(ex1)
    sums = jnp.sum(stats1[...], axis=0)
    average = sums[0:1] / D
    inverse = lax.rsqrt(sums[1:2] / D - average * average + epsilon)
    pick = iota((128, 384), 0)
    cols[...] = jnp.where(pick == 0, average, jnp.where(pick == 1, inverse, 0.0)).T
    for r in range(0, T, 64):
        v = xv[r:r + 64, :].astype(F32)
        cv[r:r + 64, :] = ((v - cols[r:r + 64, 0:1]) * cols[r:r + 64, 1:2]).astype(BF16)

    s2b = forward(g2, "yx", s2a)

    arrive(ct2)
    for s in range(NI):
        cot32[OWN * s:OWN * s + OWN, :] = unpack(cotg[s].astype(F32))
    cotb[...] = cot32[...].astype(BF16)
    cot_sum = jnp.sum(cot32[...], axis=0, keepdims=True)

    arrive(s2b)
    s3a = stage(g3, "xy")

    for f in range(0, F, 256):
        g = min(f + 256, F)
        m32[f:g, :] = lax.dot_general(
            cv[:, f:g], cotb[...], (((0,), (0,)), ((), ())), preferred_element_type=F32
        )
    spare = (iota((H, C), 0) & 31) == R
    for j in range(8):
        rows = m32[8 * R * j:8 * R * (j + 1), :].astype(BF16)
        wide = jnp.dot(spread_m[...], rows, preferred_element_type=F32)
        wide = jnp.where(spare, cot_sum, wide).astype(BF16)
        at = 2 * (j % 2)
        scat[0, j // 2, at:at + 2] = wide[:, :H].reshape(2, 4, SLOT, H)
        scat[1, j // 2, at:at + 2] = wide[:, H:].reshape(2, 4, SLOT, H)

    def sa(h, p, part):
        return scat.at[0, part_of[part], :, p] if h == 0 else scat.at[1, part_of[part], p, :]

    def sb(h, p, part):
        return scat2.at[h, part_of[part], p]

    def scatter_one(view, land, axes):
        copies = []
        for h in (0, 1):
            p = {"y": y, "x": x}[axes[h]]
            copies += [
                remote(view(h, up(p, 2), 1), land.at[h, 0], to_grp(axes[h], 1)),
                remote(view(h, up(p, 2), 2), land.at[h, 1], to_grp(axes[h], 3)),
            ]
        return start(copies)

    def scatter_two(view, land, out, axes, copies):
        second = []
        for h in (0, 1):
            p = {"y": y, "x": x}[axes[h]]
            arrive(copies[2 * h:2 * h + 2])
            for side, by in ((0, 1), (1, 3)):
                ref = view(h, up(p, by), 1 + side)
                ref[...] = (ref[...].astype(F32) + land[h, side].astype(F32)).astype(BF16)
                second += start([remote(view(h, up(p, by), 0), out.at[h, side], to_grp(axes[h], by))])
        return second

    ra = scatter_one(sa, land1, "xy")
    s3b = forward(g3, "xy", s3a)
    rb = scatter_two(sa, land1, land2, "xy", ra)
    arrive(s3b)

    extra = [jnp.zeros((8, H), F32), jnp.zeros((8, H), F32)]
    for h in (0, 1):
        for j in range(4):
            block = gath[h, j].reshape(16 * SLOT, H)
            p0 = jnp.dot(squeeze_m[...], block[:H], preferred_element_type=F32)
            p1 = jnp.dot(squeeze_m[...], block[H:], preferred_element_type=F32)
            rows = jnp.concatenate([p0[:8 * R], p1[:8 * R]], axis=0)
            wc[16 * R * j:16 * R * (j + 1), H * h:H * (h + 1)] = rows.astype(BF16)
            extra[h] = extra[h] + p0[8 * R:] + p1[8 * R:]
    extra = jnp.concatenate(extra, axis=1)
    bias_row, weight_row = extra[0:1], extra[1:2]

    part32[...] = jnp.dot(cv[...], wc[...], preferred_element_type=F32)
    cross = jnp.sum(cot32[...] * part32[...], axis=1, keepdims=True)
    plain = jnp.sum(cot32[...] * weight_row, axis=1, keepdims=True)
    lane = iota((T, 128), 1)
    st[0:T, :] = jnp.where(lane == 0, plain, jnp.where(lane == 1, cross, 0.0))
    stats2[me] = st[...].T[0:2, :]
    ex2 = start([
        remote(stats2.at[me], stats2.at[me], {"grp": grp, "intra": (me + d) % NI}) for d in range(1, NI)
    ])
    for s in range(NI):
        pown[s] = pack(part32[OWN * s:OWN * s + OWN, :] + bias_row).astype(BF16)
    exp = start([
        remote(pown.at[(me + d) % NI], pland.at[d - 1], {"grp": grp, "intra": (me + d) % NI})
        for d in range(1, NI)
    ])

    def scatter_three(view, out, axes, copies, store):
        for h in (0, 1):
            p = {"y": y, "x": x}[axes[h]]
            arrive(copies[2 * h:2 * h + 2])
            total = view(h, p, 0)[...].astype(F32) + out[h, 0].astype(F32) + out[h, 1].astype(F32)
            store(h, total.astype(BF16))

    def store2(h, value):
        scat2[h] = value

    def store3(h, value):
        scat3[h] = value

    scatter_three(sa, land2, "xy", rb, store2)
    rc = scatter_one(sb, land3, "yx")

    arrive(ex2)
    means = jnp.sum(stats2[...], axis=0) / D
    cols2[...] = jnp.where(pick == 0, means[0:1], jnp.where(pick == 1, means[1:2], 0.0)).T

    def input_part(f):
        g = min(f + 256, F)
        scaled = lax.dot_general(
            cotb[...], wc[f:g, :], (((1,), (1,)), ((), ())), preferred_element_type=F32
        )
        centred = (xv[:, f:g].astype(F32) - cols[0:T, 0:1]) * cols[0:T, 1:2]
        value = cols[0:T, 1:2] * (scaled - cols2[0:T, 0:1] - centred * cols2[0:T, 1:2])
        igv[:, f:g] = value.astype(BF16)

    for f in range(0, 1024, 256):
        input_part(f)
    rd = scatter_two(sb, land3, land4, "yx", rc)
    for f in range(1024, F, 256):
        input_part(f)
    ig_copy = pltpu.make_async_copy(igv, ig_hbm, local.at[1])
    ig_copy.start()

    scatter_three(sb, land4, "yx", rd, store3)
    re = start([
        remote(scat3.at[0, up(z, 2)], land5.at[0], to_grp("z", 1)),
        remote(scat3.at[1, up(z, 2)], land5.at[1], to_grp("z", 3)),
    ])

    arrive(exp)
    total = pown[me].astype(F32)
    for d in range(NI - 1):
        total = total + pland[d].astype(F32)
    proj_ref[...] = unpack(total).astype(BF16)

    arrive(re)
    scat3[0, up(z, 1)] = (scat3[0, up(z, 1)].astype(F32) + land5[0].astype(F32)).astype(BF16)
    scat3[1, up(z, 3)] = (scat3[1, up(z, 3)].astype(F32) + land5[1].astype(F32)).astype(BF16)
    rf = start([
        remote(scat3.at[:, up(z, 1)], land6.at[0], to_grp("z", 1)),
        remote(scat3.at[:, up(z, 3)], land6.at[1], to_grp("z", 3)),
    ])
    arrive(rf)
    halves = [
        scat3[h, z].astype(F32) + land6[0, h].astype(F32) + land6[1, h].astype(F32) for h in (0, 1)
    ]
    total = jnp.concatenate(halves, axis=1)
    sum_row = total[R:R + 1]
    weight = wfull[...]
    wg_ref[...] = (total * gain + bias * sum_row)[:R]

    def as_row(v):
        return jnp.sum(jnp.where(diagonal, v, 0.0), axis=0, keepdims=True)

    gg_ref[...] = as_row(jnp.sum(weight * total, axis=1, keepdims=True))
    bg_ref[...] = as_row(jnp.sum(weight * sum_row, axis=1, keepdims=True))

    for c in started:
        c.wait_send()
    ig_copy.wait()


def shards(activations, norm_gain, norm_bias, kv_weight, kv_cotangent):
    vmem = pl.BlockSpec(memory_space=pltpu.VMEM)
    hbm = pl.BlockSpec(memory_space=pl.ANY)

    def v16(*shape):
        return pltpu.VMEM(shape, BF16)

    def v32(*shape):
        return pltpu.VMEM(shape, F32)

    projected, input_grad, weight_grad, gain_grad, bias_grad = pl.pallas_call(
        kernel,
        out_shape=(
            jax.ShapeDtypeStruct((OWN, C), BF16),
            jax.ShapeDtypeStruct((T, F), BF16),
            jax.ShapeDtypeStruct((R, C), F32),
            jax.ShapeDtypeStruct((1, R), F32),
            jax.ShapeDtypeStruct((1, R), F32),
        ),
        in_specs=[hbm, vmem, vmem, vmem, vmem],
        out_specs=(vmem, hbm, vmem, vmem, vmem),
        scratch_shapes=[
            v16(T, F), v16(T, F), v16(T, F),
            v32(SLOT, C), v16(H, 8 * R), v16(240, H),
            v32(T, C), v16(T, C), v16(NI, 16, 1280), v32(F, C),
            v16(F, C), v32(T, C),
            v16(2, 4, 4, 4, SLOT, H), v16(2, 4, 4, 4, SLOT, H),
            v16(2, 2, 2, 4, SLOT, H), v16(2, 2, 4, 4, SLOT, H),
            v16(2, 4, 4, SLOT, H), v16(2, 2, 2, SLOT, H), v16(2, 2, 4, SLOT, H),
            v16(2, 4, SLOT, H), v16(2, SLOT, H), v16(2, 2, SLOT, H),
            v32(384, 128), v32(NI, 2, 384), v32(NI, 2, 384),
            v32(384, 128), v32(384, 128),
            v16(NI, 16, 1280), v16(NI - 1, 16, 1280),
            pltpu.SemaphoreType.DMA((COPIES,)),
            pltpu.SemaphoreType.DMA((COPIES,)),
            pltpu.SemaphoreType.DMA((2,)),
        ],
        compiler_params=pltpu.CompilerParams(
            collective_id=0, has_side_effects=True, vmem_limit_bytes=48 * 1024 * 1024
        ),
    )(activations, kv_weight, norm_gain.reshape(1, R), norm_bias.reshape(1, R), kv_cotangent)
    return projected, input_grad, weight_grad, gain_grad.reshape(R), bias_grad.reshape(R)


def solution(mesh):
    return jax.shard_map(
        shards,
        mesh=mesh,
        in_specs=(
            P("grp", "intra"),
            P(("intra", "grp")),
            P(("intra", "grp")),
            P(("intra", "grp"), None),
            P(("grp", "intra"), None),
        ),
        out_specs=(
            P(("grp", "intra"), None),
            P("grp", "intra"),
            P(("intra", "grp"), None),
            P(("intra", "grp")),
            P(("intra", "grp")),
        ),
        check_vma=False,
    )
```

time: 1070 us -> 79.4 us (0.07)
  the two profiles are of different devices: /device:TPU:320 before, /device:TPU:64 now
where the time goes in v1:
time: 79.4 us; the launch traced here: 79.1 us
  Pallas kernels  71 us (89%)
  local copies, waits for them, and re-layouts  7.43 us (9%)
    pallas_call x1, Pallas kernels, shards(): pl.pallas_call(kernel, out_shape=(jax.ShapeDtypeStruct((OWN, C), BF16), j...  71 us
    unnamed x15, local copies, waits for them, and re-layouts  7.43 us

profile of v1, /device:TPU:64, one launch (start us, length us, event | category | flops | bytes accessed | tf_op | source)
XLA Modules:
  0.0 79.1 jit_solution(18073876560350416182)
XLA Ops:
  0.6 0.0 copy-start
  0.6 1.3 %copy-done = bf16[320,1856]{1,0:T(8,128)(2,1)S(1)} copy-done((bf16[320,1856]{1,0:T(8,128)(2,1)S(1)}, bf16[320,1856]{1,0:T(8,128)(2,1)}, u32[]{:S(2)}) %copy-start) | copy-done | bytes 1187864
  1.9 0.0 copy-start.1
  1.9 0.8 copy-done.1
  2.7 0.0 copy-start.2
  2.7 0.8 copy-done.2
  3.5 0.0 copy-start.3
  3.5 0.7 copy-done.3
  4.1 0.0 copy-start.4
  4.1 0.7 copy-done.4
  4.8 71.0 %shard_map.92 = (bf16[40,512]{1,0:T(8,128)(2,1)S(1)}, bf16[320,1856]{1,0:T(8,128)(2,1)S(1)}, f32[29,512]{1,0:T(8,128)S(1)}, f32[1,29]{1,0:T(1,128)S(1)}, f32[1,29]{1,0:T(1,128)S(1)}) custom-call(bf16[320,1856]{1,0:T(8,128)(2,1)S(1)} %copy-done, bf16[29,512]{1,0:T(8,128)(2,1)S(1)} %copy-done.2, bf16[1,29]{1,0:T(2,128)(2,1)S(1)} %bitcast.4, ...), custom_call_target="tpu_custom_call" | custom-call | tf_op jit(solution)/shard_map/pallas_call | solution.py:367
  75.7 0.6 copy.15
  76.4 1.0 %copy.16 = bf16[320,1856]{1,0:T(8,128)(2,1)} copy(bf16[320,1856]{1,0:T(8,128)(2,1)S(1)} %get-tuple-element.21) | data formatting | bytes 2375680
  77.4 0.6 copy.17
  78.0 0.5 copy.18
  78.5 0.5 copy.19
Async XLA Ops:
  0.6 1.3 %copy-start = (bf16[320,1856]{1,0:T(8,128)(2,1)S(1)}, bf16[320,1856]{1,0:T(8,128)(2,1)}, u32[]{:S(2)}) copy-start(bf16[320,1856]{1,0:T(8,128)(2,1)} %x_hbm.1) | copy-start | bytes 3563524
  1.9 0.8 copy-start.1
  2.7 0.8 copy-start.2
  3.5 0.7 copy-start.3
  4.1 0.7 copy-start.4

commit v2 on v1

v2 whole, which is shorter than its diff:
```python
import jax
import jax.numpy as jnp
from jax import lax
from jax.experimental import pallas as pl
from jax.experimental.pallas import tpu as pltpu
from jax.sharding import PartitionSpec as P

epsilon = 1e-05
F32, BF16 = jnp.float32, jnp.bfloat16
MESH = pl.DeviceIdType.MESH

T = 320
F = 1856
C = 512
H = 256
R = 29
SLOT = 32
OWN = 40
NI = 8
D = F * NI
COPIES = 140


def pack(v):
    tail = jnp.concatenate([v[32:40, :H], v[32:40, H:]], axis=0)
    return jnp.concatenate([v[0:16], v[16:32], tail], axis=1)


def unpack(v):
    tail = jnp.concatenate([v[0:8, 1024:], v[8:16, 1024:]], axis=1)
    return jnp.concatenate([v[:, :C], v[:, C:1024], tail], axis=0)


def iota(shape, dim):
    return lax.broadcasted_iota(jnp.int32, shape, dim)


def kernel(
    x_hbm, w_hbm, gain_hbm, bias_hbm, cot_hbm,
    proj_ref, ig_hbm, wg_ref, gg_ref, bg_ref,
    xv, w_ref, gain_ref, bias_ref, cot_ref, cv, igv, wfull, spread_m, squeeze_m,
    cot32, cotb, cotg, m32, wc, part32,
    gath, scat, land1, land2, scat2, land3, land4, scat3, land5, land6,
    st, stats1, stats2, cols, cols2, pown, pland,
    sends, recvs, local,
):
    grp, me = lax.axis_index("grp"), lax.axis_index("intra")
    z, y, x = grp // 16, (grp // 4) % 4, grp % 4
    core = me % 2

    def up(v, by):
        return (v + by) % 4

    def to_grp(axis, by):
        if axis == "z":
            return {"grp": up(z, by) * 16 + y * 4 + x, "intra": me}
        if axis == "y":
            return {"grp": z * 16 + up(y, by) * 4 + x, "intra": me}
        return {"grp": z * 16 + y * 4 + up(x, by), "intra": me}

    def to_intra(d):
        return {"grp": grp, "intra": (me + d) % NI}

    count = [0]

    def remote(src, dst, device):
        k = count[0]
        count[0] += 1
        return pltpu.make_async_remote_copy(
            src_ref=src, dst_ref=dst, send_sem=sends.at[k], recv_sem=recvs.at[k],
            device_id=device, device_id_type=MESH,
        )

    started = []

    def start(copies):
        for c in copies:
            c.start()
            started.append(c)
        return copies

    def arrive(copies):
        for c in copies:
            c.wait_recv()

    loads = [
        pltpu.make_async_copy(src, dst, local.at[k])
        for k, (src, dst) in enumerate((
            (w_hbm, w_ref), (gain_hbm, gain_ref), (bias_hbm, bias_ref), (cot_hbm, cot_ref), (x_hbm, xv),
        ))
    ]
    for load in loads:
        load.start()

    mate = {"grp": grp, "intra": me + 1 - 2 * core}
    peers = [to_grp(a, by) for a in "zyx" for by in (1, 3)] + [to_intra(d) for d in range(1, NI)]
    barrier = pltpu.get_barrier_semaphore()
    for peer in peers:
        pl.semaphore_signal(barrier, inc=1, device_id=peer, device_id_type=MESH)

    plane_of = (z, up(z, 3), up(z, 1), up(z, 2))
    groups = (slice(0, 1), slice(1, 3), slice(3, 4))

    for load in loads[:4]:
        load.wait()
    diagonal = iota((SLOT, R), 0) == iota((SLOT, R), 1)

    def column(ref):
        row = ref[...].astype(F32)
        return jnp.sum(jnp.where(diagonal, row, 0.0), axis=1, keepdims=True)

    gain, bias = column(gain_ref), column(bias_ref)
    wfull[...] = jnp.zeros_like(wfull)
    wfull[0:R, :] = w_ref[...].astype(F32)
    weight = wfull[...]
    product = jnp.sum(weight * bias, axis=0, keepdims=True)
    high = product.astype(BF16).astype(F32)
    row = iota((SLOT, C), 0)
    slot = jnp.where(row == R, high, jnp.where(row == R + 1, product - high, weight * gain)).astype(BF16)
    gath[0, 0, y, x] = slot[:, :H]
    gath[1, 0, y, x] = slot[:, H:]
    cotg[me] = pack(cot_ref[...].astype(F32)).astype(BF16)

    a, b = iota((H, 8 * R), 0), iota((H, 8 * R), 1)
    spread_m[...] = jnp.where(((a & 31) < R) & (b == R * (a >> 5) + (a & 31)), 1.0, 0.0).astype(BF16)
    a, b = iota((240, H), 0), iota((240, H), 1)
    within = b & 31
    hit = (within < R) & ((a == R * (b >> 5) + within) | (a == 233))
    hit = hit | ((within >= R) & (within < R + 2) & (a == 232))
    squeeze_m[...] = jnp.where(hit, 1.0, 0.0).astype(BF16)

    pl.semaphore_wait(barrier, len(peers))

    place = {"y": y, "x": x}
    whole, pairs, halves16 = slice(None), (slice(0, 2), slice(2, 4)), (slice(0, 16), slice(16, 32))

    def row_block(h, g, p, part):
        return gath.at[0, groups[g], p, x, part] if h == 0 else gath.at[1, groups[g], y, p, part]

    def plane_block(h, g, p, part):
        return gath.at[0, groups[g], part, p] if h == 0 else gath.at[1, groups[g], p, part]

    def ring_own(view, axes, g):
        copies = []
        for h in (0, 1):
            ref = view(h, g, place[axes[h]], whole)
            copies += [remote(ref, ref, to_grp(axes[h], by)) for by in (1, 3)]
        return start(copies)

    def ring_next(view, axes, parts, g, first):
        copies = []
        for h in (0, 1):
            p = place[axes[h]]
            arrive(first[2 * h:2 * h + 2])
            low, top = view(h, g, up(p, 3), parts[0]), view(h, g, up(p, 1), parts[1])
            copies += start([remote(low, low, to_grp(axes[h], 1)), remote(top, top, to_grp(axes[h], 3))])
        return copies

    def rows_own(g):
        return ring_own(row_block, "yx", g)

    def rows_next(g, first):
        return ring_next(row_block, "yx", halves16, g, first)

    def planes_own(g):
        return ring_own(plane_block, "xy", g)

    def planes_next(g, first):
        return ring_next(plane_block, "xy", pairs, g, first)

    gz1 = start([
        remote(gath.at[:, 0, y, x], gath.at[:, 1, y, x], to_grp("z", 1)),
        remote(gath.at[:, 0, y, x], gath.at[:, 2, y, x], to_grp("z", 3)),
    ])
    a0 = rows_own(0)
    ct1 = start([remote(cotg.at[me], cotg.at[me], mate)])
    ct1 += start([remote(cotg.at[me], cotg.at[me], to_intra(d)) for d in (2, 6, 4)])

    loads[4].wait()
    st[...] = jnp.zeros_like(st)
    lane = iota((64, 128), 1)
    for r in range(0, T, 64):
        v = xv[r:r + 64, :].astype(F32)
        s1 = jnp.sum(v, axis=1, keepdims=True)
        s2 = jnp.sum(v * v, axis=1, keepdims=True)
        st[r:r + 64, :] = jnp.where(lane == 0, s1, jnp.where(lane == 1, s2, 0.0))
    stats1[me] = st[...].T[0:2, :]
    ex1 = start([remote(stats1.at[me], stats1.at[me], to_intra(d)) for d in range(1, NI)])

    b0 = rows_next(0, a0)
    arrive(b0)
    c0 = planes_own(0)

    arrive(ex1)
    sums = jnp.sum(stats1[...], axis=0)
    average = sums[0:1] / D
    inverse = lax.rsqrt(sums[1:2] / D - average * average + epsilon)
    pick = iota((128, 384), 0)
    cols[...] = jnp.where(pick == 0, average, jnp.where(pick == 1, inverse, 0.0)).T
    for r in range(0, T, 64):
        v = xv[r:r + 64, :].astype(F32)
        cv[r:r + 64, :] = ((v - cols[r:r + 64, 0:1]) * cols[r:r + 64, 1:2]).astype(BF16)

    arrive(gz1)
    gz2 = start([
        remote(gath.at[0, 1, y, x], gath.at[0, 3, y, x], to_grp("z", 1)),
        remote(gath.at[1, 2, y, x], gath.at[1, 3, y, x], to_grp("z", 3)),
    ])
    a1 = rows_own(1)
    d0 = planes_next(0, c0)
    b1 = rows_next(1, a1)
    arrive(ct1)
    ct2 = start([remote(cotg.at[(me + d) % NI], cotg.at[(me + d) % NI], mate) for d in (6, 2, 4)])
    arrive(gz2)
    a2 = rows_own(2)
    arrive(b1)
    c1 = planes_own(1)
    b2 = rows_next(2, a2)

    arrive(ct2)
    for s in range(NI):
        cot32[OWN * s:OWN * s + OWN, :] = unpack(cotg[s].astype(F32))
    cotb[...] = cot32[...].astype(BF16)
    cot_sum = jnp.sum(cot32[...], axis=0, keepdims=True)

    arrive(b2)
    c2 = planes_own(2)

    for f in range(0, F, 256):
        g = min(f + 256, F)
        m32[f:g, :] = lax.dot_general(
            cv[:, f:g], cotb[...], (((0,), (0,)), ((), ())), preferred_element_type=F32
        )
    spare = (iota((H, C), 0) & 31) == R

    def spread(s):
        for j in range(2):
            base = pl.multiple_of(16 * R * plane_of[s] + 8 * R * j, 8)
            rows = m32[pl.ds(base, 8 * R), :].astype(BF16)
            wide = jnp.dot(spread_m[...], rows, preferred_element_type=F32)
            wide = jnp.where(spare, cot_sum, wide).astype(BF16)
            scat[0, s, 2 * j:2 * j + 2] = wide[:, :H].reshape(2, 4, SLOT, H)
            scat[1, s, 2 * j:2 * j + 2] = wide[:, H:].reshape(2, 4, SLOT, H)

    def plane_part(h, g, p, part):
        return scat.at[0, groups[g], part, p] if h == 0 else scat.at[1, groups[g], p, part]

    def row_part(h, g, p, part):
        return scat2.at[h, groups[g], p, part]

    def part_far(view, land, axes, parts, g):
        copies = []
        for h in (0, 1):
            far = up(place[axes[h]], 2)
            copies += [
                remote(view(h, g, far, parts[side]), land.at[h, side, groups[g]], to_grp(axes[h], by))
                for side, by in ((0, 1), (1, 3))
            ]
        return start(copies)

    def part_near(view, land, out, axes, parts, g, first):
        copies = []
        for h in (0, 1):
            arrive(first[2 * h:2 * h + 2])
            for side, by in ((0, 1), (1, 3)):
                near = up(place[axes[h]], by)
                ref = view(h, g, near, parts[side])
                ref[...] = (ref[...].astype(F32) + land[h, side, groups[g]].astype(F32)).astype(BF16)
                copies += start([remote(view(h, g, near, whole), out.at[h, side, groups[g]], to_grp(axes[h], by))])
        return copies

    def part_sum(view, out, axes, g, second, h):
        arrive(second[2 * h:2 * h + 2])
        total = view(h, g, place[axes[h]], whole)[...].astype(F32)
        return total + out[h, 0, groups[g]].astype(F32) + out[h, 1, groups[g]].astype(F32)

    def planes_far(g):
        return part_far(plane_part, land1, "xy", pairs, g)

    def planes_near(g, first):
        return part_near(plane_part, land1, land2, "xy", pairs, g, first)

    def planes_sum(g, second):
        for h in (0, 1):
            scat2[h, groups[g]] = part_sum(plane_part, land2, "xy", g, second, h).astype(BF16)

    def rows_far(g):
        return part_far(row_part, land3, "yx", halves16, g)

    def rows_near(g, first):
        return part_near(row_part, land3, land4, "yx", halves16, g, first)

    def rows_sum(g, second):
        for h in (0, 1):
            scat3[h, groups[g]] = part_sum(row_part, land4, "yx", g, second, h).astype(BF16)

    spread(3)
    e2 = planes_far(2)
    spread(1)
    spread(2)
    d1 = planes_next(1, c1)
    e1 = planes_far(1)
    spread(0)
    f2 = planes_near(2, e2)
    d2 = planes_next(2, c2)
    e0 = planes_far(0)

    extra = [jnp.zeros((8, H), F32), jnp.zeros((8, H), F32)]

    def squeeze(s):
        for h in (0, 1):
            block = gath[h, s].reshape(16 * SLOT, H)
            p0 = jnp.dot(squeeze_m[...], block[:H], preferred_element_type=F32)
            p1 = jnp.dot(squeeze_m[...], block[H:], preferred_element_type=F32)
            rows = jnp.concatenate([p0[:8 * R], p1[:8 * R]], axis=0)
            base = pl.multiple_of(16 * R * plane_of[s], 16)
            wc[pl.ds(base, 16 * R), H * h:H * (h + 1)] = rows.astype(BF16)
            extra[h] = extra[h] + p0[8 * R:] + p1[8 * R:]

    arrive(d0)
    squeeze(0)
    f1 = planes_near(1, e1)
    arrive(d1)
    squeeze(1)
    squeeze(2)
    planes_sum(2, f2)
    g2 = rows_far(2)
    arrive(d2)
    squeeze(3)
    extra = jnp.concatenate(extra, axis=1)
    bias_row, weight_row = extra[0:1], extra[1:2]
    f0 = planes_near(0, e0)

    part32[...] = jnp.dot(cv[...], wc[...], preferred_element_type=F32)
    cross = jnp.sum(cot32[...] * part32[...], axis=1, keepdims=True)
    plain = jnp.sum(cot32[...] * weight_row, axis=1, keepdims=True)
    lane = iota((T, 128), 1)
    st[0:T, :] = jnp.where(lane == 0, plain, jnp.where(lane == 1, cross, 0.0))
    stats2[me] = st[...].T[0:2, :]
    ex2 = start([remote(stats2.at[me], stats2.at[me], to_intra(d)) for d in range(1, NI)])
    h2 = rows_near(2, g2)
    for s in range(NI):
        pown[s] = pack(part32[OWN * s:OWN * s + OWN, :] + bias_row).astype(BF16)
    exp = start([remote(pown.at[(me + d) % NI], pland.at[d - 1], to_intra(d)) for d in range(1, NI)])

    planes_sum(1, f1)
    g1 = rows_far(1)
    rows_sum(2, h2)
    rz1 = start([
        remote(scat3.at[0, 3], land5.at[0], to_grp("z", 1)),
        remote(scat3.at[1, 3], land5.at[1], to_grp("z", 3)),
    ])

    arrive(ex2)
    means = jnp.sum(stats2[...], axis=0) / D
    cols2[...] = jnp.where(pick == 0, means[0:1], jnp.where(pick == 1, means[1:2], 0.0)).T

    def input_part(f):
        g = min(f + 256, F)
        scaled = lax.dot_general(
            cotb[...], wc[f:g, :], (((1,), (1,)), ((), ())), preferred_element_type=F32
        )
        centred = (xv[:, f:g].astype(F32) - cols[0:T, 0:1]) * cols[0:T, 1:2]
        value = cols[0:T, 1:2] * (scaled - cols2[0:T, 0:1] - centred * cols2[0:T, 1:2])
        igv[:, f:g] = value.astype(BF16)

    for f in range(0, 1024, 256):
        input_part(f)
    planes_sum(0, f0)
    g0 = rows_far(0)
    h1 = rows_near(1, g1)
    for f in range(1024, F, 256):
        input_part(f)
    ig_copy = pltpu.make_async_copy(igv, ig_hbm, local.at[0])
    ig_copy.start()

    h0 = rows_near(0, g0)
    rows_sum(1, h1)
    arrive(rz1)
    scat3[0, 2] = (scat3[0, 2].astype(F32) + land5[0].astype(F32)).astype(BF16)
    scat3[1, 1] = (scat3[1, 1].astype(F32) + land5[1].astype(F32)).astype(BF16)
    rz2 = start([
        remote(scat3.at[:, 2], land6.at[0], to_grp("z", 1)),
        remote(scat3.at[:, 1], land6.at[1], to_grp("z", 3)),
    ])

    arrive(exp)
    total = pown[me].astype(F32)
    for d in range(NI - 1):
        total = total + pland[d].astype(F32)
    proj_ref[...] = unpack(total).astype(BF16)

    mine = [part_sum(row_part, land4, "yx", 0, h0, h)[0] for h in (0, 1)]
    arrive(rz2)
    total = jnp.concatenate([
        mine[h] + land6[0, h].astype(F32) + land6[1, h].astype(F32) for h in (0, 1)
    ], axis=1)
    sum_row = total[R:R + 1]
    weight = wfull[...]
    wg_ref[...] = (total * gain + bias * sum_row)[:R]

    def as_row(v):
        return jnp.sum(jnp.where(diagonal, v, 0.0), axis=0, keepdims=True)

    gg_ref[...] = as_row(jnp.sum(weight * total, axis=1, keepdims=True))
    bg_ref[...] = as_row(jnp.sum(weight * sum_row, axis=1, keepdims=True))

    for c in started:
        c.wait_send()
    ig_copy.wait()


def writer(a, b, c, d, e, a_out, b_out, c_out, d_out, e_out, av, bv, cv, dv, ev, taken, given):
    tasks = [(b.at[r:r + 80], bv.at[r:r + 80], b_out.at[r:r + 80]) for r in range(0, T, 80)]
    tasks += [(a, av, a_out), (c, cv, c_out), (d, dv, d_out), (e, ev, e_out)]
    reads = [pltpu.make_async_copy(s, v, taken.at[k]) for k, (s, v, _) in enumerate(tasks)]
    writes = [pltpu.make_async_copy(v, o, given.at[k]) for k, (_, v, o) in enumerate(tasks)]
    for read in reads:
        read.start()
    for read, write in zip(reads, writes):
        read.wait()
        write.start()
    for write in writes:
        write.wait()


def shards(activations, norm_gain, norm_bias, kv_weight, kv_cotangent):
    vmem = pl.BlockSpec(memory_space=pltpu.VMEM)
    hbm = pl.BlockSpec(memory_space=pltpu.HBM)

    def v16(*shape):
        return pltpu.VMEM(shape, BF16)

    def v32(*shape):
        return pltpu.VMEM(shape, F32)

    shapes = (
        jax.ShapeDtypeStruct((OWN, C), BF16),
        jax.ShapeDtypeStruct((T, F), BF16),
        jax.ShapeDtypeStruct((R, C), F32),
        jax.ShapeDtypeStruct((1, R), F32),
        jax.ShapeDtypeStruct((1, R), F32),
    )
    results = pl.pallas_call(
        kernel,
        out_shape=shapes,
        in_specs=[hbm] * 5,
        out_specs=(vmem, hbm, vmem, vmem, vmem),
        scratch_shapes=[
            v16(T, F), v16(R, C), v16(1, R), v16(1, R), v16(OWN, C),
            v16(T, F), v16(T, F),
            v32(SLOT, C), v16(H, 8 * R), v16(240, H),
            v32(T, C), v16(T, C), v16(NI, 16, 1280), v32(F, C),
            v16(F, C), v32(T, C),
            v16(2, 4, 4, 4, SLOT, H), v16(2, 4, 4, 4, SLOT, H),
            v16(2, 2, 4, 2, SLOT, H), v16(2, 2, 4, 4, SLOT, H),
            v16(2, 4, 4, SLOT, H), v16(2, 2, 4, 16, H), v16(2, 2, 4, SLOT, H),
            v16(2, 4, SLOT, H), v16(2, SLOT, H), v16(2, 2, SLOT, H),
            v32(384, 128), v32(NI, 2, 384), v32(NI, 2, 384),
            v32(384, 128), v32(384, 128),
            v16(NI, 16, 1280), v16(NI - 1, 16, 1280),
            pltpu.SemaphoreType.DMA((COPIES,)),
            pltpu.SemaphoreType.DMA((COPIES,)),
            pltpu.SemaphoreType.DMA((5,)),
        ],
        compiler_params=pltpu.CompilerParams(
            collective_id=0, has_side_effects=True, vmem_limit_bytes=60 * 1024 * 1024
        ),
    )(activations, kv_weight, norm_gain.reshape(1, R), norm_bias.reshape(1, R), kv_cotangent)
    anywhere = pl.BlockSpec(memory_space=pl.ANY)
    projected, input_grad, weight_grad, gain_grad, bias_grad = pl.pallas_call(
        writer,
        out_shape=shapes,
        in_specs=[anywhere] * 5,
        out_specs=(hbm,) * 5,
        scratch_shapes=[
            v16(OWN, C), v16(T, F), v32(R, C), v32(1, R), v32(1, R),
            pltpu.SemaphoreType.DMA((8,)), pltpu.SemaphoreType.DMA((8,)),
        ],
        compiler_params=pltpu.CompilerParams(vmem_limit_bytes=60 * 1024 * 1024),
    )(*results)
    return projected, input_grad, weight_grad, gain_grad.reshape(R), bias_grad.reshape(R)


def solution(mesh):
    return jax.shard_map(
        shards,
        mesh=mesh,
        in_specs=(
            P("grp", "intra"),
            P(("intra", "grp")),
            P(("intra", "grp")),
            P(("intra", "grp"), None),
            P(("grp", "intra"), None),
        ),
        out_specs=(
            P(("grp", "intra"), None),
            P("grp", "intra"),
            P(("intra", "grp"), None),
            P(("intra", "grp")),
            P(("intra", "grp")),
        ),
        check_vma=False,
    )
```

time: 79.4 us -> 68.1 us (0.86)
  the two profiles are of different devices: /device:TPU:64 before, /device:TPU:32 now
where the time goes in v2:
time: 68.1 us; the launch traced here: 68 us
  Pallas kernels  67.3 us (99%)
    pallas_call x1, Pallas kernels, shards(): pl.pallas_call(kernel, out_shape=shapes, in_specs=[hbm] * 5, out_specs=(v...  65.2 us
    pallas_call x1, Pallas kernels, shards(): pl.pallas_call(writer, out_shape=shapes, in_specs=[anywhere] * 5, out_spe...  2.16 us

profile of v2, /device:TPU:32, one launch (start us, length us, event | category | flops | bytes accessed | tf_op | source)
XLA Modules:
  0.0 68.0 jit_solution(408458624129615275)
XLA Ops:
  0.6 65.2 %shard_map.92 = (bf16[40,512]{1,0:T(8,128)(2,1)}, bf16[320,1856]{1,0:T(8,128)(2,1)}, f32[29,512]{1,0:T(8,128)}, f32[1,29]{1,0:T(1,128)}, f32[1,29]{1,0:T(1,128)}) custom-call(bf16[320,1856]{1,0:T(8,128)(2,1)} %x_hbm.1, bf16[29,512]{1,0:T(8,128)(2,1)} %w_hbm.1, bf16[1,29]{1,0:T(2,128)(2,1)} %bitcast.4, bf16[1,29]{1,0:T(2,128)(2,1)} %bitcast.5, ...), custom_call_target="tpu_custom_call" | custom-call | tf_op jit(solution)/shard_map/pallas_call | solution.py:444
  65.8 2.2 %shard_map.93 = (bf16[40,512]{1,0:T(8,128)(2,1)}, bf16[320,1856]{1,0:T(8,128)(2,1)}, f32[29,512]{1,0:T(8,128)}, f32[1,29]{1,0:T(1,128)}, f32[1,29]{1,0:T(1,128)}) custom-call(bf16[40,512]{1,0:T(8,128)(2,1)} %get-tuple-element.15.a, bf16[320,1856]{1,0:T(8,128)(2,1)} %get-tuple-element.16.b, f32[29,512]{1,0:T(8,128)} %get-tuple-element.17.c, ...), custom_call_target="tpu_custom_call" | custom-call | tf_op jit(solution)/shard_map/pallas_call | solution.py:471

commit v3 on v2

--- a/solution.py
+++ b/solution.py
@@ -19,6 +19,8 @@
 NI = 8
 D = F * NI
 COPIES = 140
+GATHER_DIRECT = (False, False, True)
+SCATTER_DIRECT = (False, False, False)
 
 
 def pack(v):
@@ -40,8 +42,8 @@
     proj_ref, ig_hbm, wg_ref, gg_ref, bg_ref,
     xv, w_ref, gain_ref, bias_ref, cot_ref, cv, igv, wfull, spread_m, squeeze_m,
     cot32, cotb, cotg, m32, wc, part32,
-    gath, scat, land1, land2, scat2, land3, land4, scat3, land5, land6,
-    st, stats1, stats2, cols, cols2, pown, pland,
+    gath, scat, land1, land2, scat2, land4, scat3, land5, land6,
+    st, stats1, stats2, cols, cols2, pown, pmate, psum, pland,
     sends, recvs, local,
 ):
     grp, me = lax.axis_index("grp"), lax.axis_index("intra")
@@ -78,6 +80,11 @@
             c.start()
             started.append(c)
         return copies
+
+    def drain(n):
+        for c in started[:n]:
+            c.wait_send()
+        del started[:n]
 
     def arrive(copies):
         for c in copies:
@@ -93,7 +100,7 @@
         load.start()
 
     mate = {"grp": grp, "intra": me + 1 - 2 * core}
-    peers = [to_grp(a, by) for a in "zyx" for by in (1, 3)] + [to_intra(d) for d in range(1, NI)]
+    peers = [to_grp(a, by) for a in "zyx" for by in (1, 2, 3)] + [to_intra(d) for d in range(1, NI)]
     barrier = pltpu.get_barrier_semaphore()
     for peer in peers:
         pl.semaphore_signal(barrier, inc=1, device_id=peer, device_id_type=MESH)
@@ -101,7 +108,7 @@
     plane_of = (z, up(z, 3), up(z, 1), up(z, 2))
     groups = (slice(0, 1), slice(1, 3), slice(3, 4))
 
-    for load in loads[:4]:
+    for load in loads[:3]:
         load.wait()
     diagonal = iota((SLOT, R), 0) == iota((SLOT, R), 1)
 
@@ -119,20 +126,11 @@
     slot = jnp.where(row == R, high, jnp.where(row == R + 1, product - high, weight * gain)).astype(BF16)
     gath[0, 0, y, x] = slot[:, :H]
     gath[1, 0, y, x] = slot[:, H:]
-    cotg[me] = pack(cot_ref[...].astype(F32)).astype(BF16)
-
-    a, b = iota((H, 8 * R), 0), iota((H, 8 * R), 1)
-    spread_m[...] = jnp.where(((a & 31) < R) & (b == R * (a >> 5) + (a & 31)), 1.0, 0.0).astype(BF16)
-    a, b = iota((240, H), 0), iota((240, H), 1)
-    within = b & 31
-    hit = (within < R) & ((a == R * (b >> 5) + within) | (a == 233))
-    hit = hit | ((within >= R) & (within < R + 2) & (a == 232))
-    squeeze_m[...] = jnp.where(hit, 1.0, 0.0).astype(BF16)
 
     pl.semaphore_wait(barrier, len(peers))
 
     place = {"y": y, "x": x}
-    whole, pairs, halves16 = slice(None), (slice(0, 2), slice(2, 4)), (slice(0, 16), slice(16, 32))
+    whole, pairs = slice(None), (slice(0, 2), slice(2, 4))
 
     def row_block(h, g, p, part):
         return gath.at[0, groups[g], p, x, part] if h == 0 else gath.at[1, groups[g], y, p, part]
@@ -140,11 +138,11 @@
     def plane_block(h, g, p, part):
         return gath.at[0, groups[g], part, p] if h == 0 else gath.at[1, groups[g], p, part]
 
-    def ring_own(view, axes, g):
+    def ring_own(view, axes, g, direct):
         copies = []
         for h in (0, 1):
             ref = view(h, g, place[axes[h]], whole)
-            copies += [remote(ref, ref, to_grp(axes[h], by)) for by in (1, 3)]
+            copies += [remote(ref, ref, to_grp(axes[h], by)) for by in ((1, 3, 2) if direct else (1, 3))]
         return start(copies)
 
     def ring_next(view, axes, parts, g, first):
@@ -157,24 +155,22 @@
         return copies
 
     def rows_own(g):
-        return ring_own(row_block, "yx", g)
-
-    def rows_next(g, first):
-        return ring_next(row_block, "yx", halves16, g, first)
+        return ring_own(row_block, "yx", g, True)
 
     def planes_own(g):
-        return ring_own(plane_block, "xy", g)
+        return ring_own(plane_block, "xy", g, GATHER_DIRECT[g])
 
     def planes_next(g, first):
-        return ring_next(plane_block, "xy", pairs, g, first)
-
-    gz1 = start([
-        remote(gath.at[:, 0, y, x], gath.at[:, 1, y, x], to_grp("z", 1)),
-        remote(gath.at[:, 0, y, x], gath.at[:, 2, y, x], to_grp("z", 3)),
-    ])
+        return first if GATHER_DIRECT[g] else ring_next(plane_block, "xy", pairs, g, first)
+
+    def own_to(slot, by):
+        return start([remote(gath.at[:, 0, y, x], gath.at[:, slot, y, x], to_grp("z", by))])
+
+    gz1 = own_to(1, 1) + own_to(2, 3)
     a0 = rows_own(0)
-    ct1 = start([remote(cotg.at[me], cotg.at[me], mate)])
-    ct1 += start([remote(cotg.at[me], cotg.at[me], to_intra(d)) for d in (2, 6, 4)])
+    loads[3].wait()
+    cotg[me] = pack(cot_ref[...].astype(F32)).astype(BF16)
+    ct0 = start([remote(cotg.at[me], cotg.at[me], mate)])
 
     loads[4].wait()
     st[...] = jnp.zeros_like(st)
@@ -187,9 +183,20 @@
     stats1[me] = st[...].T[0:2, :]
     ex1 = start([remote(stats1.at[me], stats1.at[me], to_intra(d)) for d in range(1, NI)])
 
-    b0 = rows_next(0, a0)
-    arrive(b0)
+    a, b = iota((H, 8 * R), 0), iota((H, 8 * R), 1)
+    spread_m[...] = jnp.where(((a & 31) < R) & (b == R * (a >> 5) + (a & 31)), 1.0, 0.0).astype(BF16)
+    a, b = iota((240, H), 0), iota((240, H), 1)
+    within = b & 31
+    hit = (within < R) & ((a == R * (b >> 5) + within) | (a == 233))
+    hit = hit | ((within >= R) & (within < R + 2) & (a == 232))
+    squeeze_m[...] = jnp.where(hit, 1.0, 0.0).astype(BF16)
+
+    arrive(a0)
     c0 = planes_own(0)
+    for c in gz1:
+        c.wait_send()
+    del started[:2]
+    ct1 = start([remote(cotg.at[me], cotg.at[me], to_intra(d)) for d in (2, 6, 4)])
 
     arrive(ex1)
     sums = jnp.sum(stats1[...], axis=0)
@@ -208,23 +215,18 @@
     ])
     a1 = rows_own(1)
     d0 = planes_next(0, c0)
-    b1 = rows_next(1, a1)
+    arrive(a1)
+    c1 = planes_own(1)
     arrive(ct1)
     ct2 = start([remote(cotg.at[(me + d) % NI], cotg.at[(me + d) % NI], mate) for d in (6, 2, 4)])
     arrive(gz2)
     a2 = rows_own(2)
-    arrive(b1)
-    c1 = planes_own(1)
-    b2 = rows_next(2, a2)
-
+    arrive(ct0)
     arrive(ct2)
     for s in range(NI):
         cot32[OWN * s:OWN * s + OWN, :] = unpack(cotg[s].astype(F32))
     cotb[...] = cot32[...].astype(BF16)
     cot_sum = jnp.sum(cot32[...], axis=0, keepdims=True)
-
-    arrive(b2)
-    c2 = planes_own(2)
 
     for f in range(0, F, 256):
         g = min(f + 256, F)
@@ -248,14 +250,20 @@
     def row_part(h, g, p, part):
         return scat2.at[h, groups[g], p, part]
 
-    def part_far(view, land, axes, parts, g):
+    def part_far(view, land, out, axes, parts, g, direct):
         copies = []
         for h in (0, 1):
-            far = up(place[axes[h]], 2)
-            copies += [
-                remote(view(h, g, far, parts[side]), land.at[h, side, groups[g]], to_grp(axes[h], by))
-                for side, by in ((0, 1), (1, 3))
-            ]
+            p = place[axes[h]]
+            if direct:
+                copies += [
+                    remote(view(h, g, up(p, by), whole), out.at[h, k, groups[g]], to_grp(axes[h], by))
+                    for k, by in enumerate((1, 3, 2))
+                ]
+            else:
+                copies += [
+                    remote(view(h, g, up(p, 2), parts[k]), land.at[h, k, groups[g]], to_grp(axes[h], by))
+                    for k, by in enumerate((1, 3))
+                ]
         return start(copies)
 
     def part_near(view, land, out, axes, parts, g, first):
@@ -269,41 +277,45 @@
                 copies += start([remote(view(h, g, near, whole), out.at[h, side, groups[g]], to_grp(axes[h], by))])
         return copies
 
-    def part_sum(view, out, axes, g, second, h):
-        arrive(second[2 * h:2 * h + 2])
+    def part_sum(view, out, axes, g, last, h):
+        n = len(last) // 2
+        arrive(last[n * h:n * h + n])
         total = view(h, g, place[axes[h]], whole)[...].astype(F32)
-        return total + out[h, 0, groups[g]].astype(F32) + out[h, 1, groups[g]].astype(F32)
+        for k in range(n):
+            total = total + out[h, k, groups[g]].astype(F32)
+        return total
 
     def planes_far(g):
-        return part_far(plane_part, land1, "xy", pairs, g)
+        return part_far(plane_part, land1, land2, "xy", pairs, g, SCATTER_DIRECT[g])
 
     def planes_near(g, first):
-        return part_near(plane_part, land1, land2, "xy", pairs, g, first)
-
-    def planes_sum(g, second):
-        for h in (0, 1):
-            scat2[h, groups[g]] = part_sum(plane_part, land2, "xy", g, second, h).astype(BF16)
+        return first if SCATTER_DIRECT[g] else part_near(plane_part, land1, land2, "xy", pairs, g, first)
+
+    def planes_sum(g, last):
+        for h in (0, 1):
+            scat2[h, groups[g]] = part_sum(plane_part, land2, "xy", g, last, h).astype(BF16)
 
     def rows_far(g):
-        return part_far(row_part, land3, "yx", halves16, g)
-
-    def rows_near(g, first):
-        return part_near(row_part, land3, land4, "yx", halves16, g, first)
-
-    def rows_sum(g, second):
-        for h in (0, 1):
-            scat3[h, groups[g]] = part_sum(row_part, land4, "yx", g, second, h).astype(BF16)
+        return part_far(row_part, None, land4, "yx", None, g, True)
+
+    def rows_sum(g, last):
+        for h in (0, 1):
+            scat3[h, groups[g]] = part_sum(row_part, land4, "yx", g, last, h).astype(BF16)
+
+    def scatter_to(slot, by):
+        return start([remote(scat3.at[:, slot], land6.at[slot - 1], to_grp("z", by))])
 
     spread(3)
     e2 = planes_far(2)
+    arrive(a2)
+    c2 = planes_own(2)
     spread(1)
     spread(2)
+    e1 = planes_far(1)
     d1 = planes_next(1, c1)
-    e1 = planes_far(1)
     spread(0)
     f2 = planes_near(2, e2)
-    d2 = planes_next(2, c2)
-    e0 = planes_far(0)
+    drain(30)
 
     extra = [jnp.zeros((8, H), F32), jnp.zeros((8, H), F32)]
 
@@ -319,7 +331,9 @@
 
     arrive(d0)
     squeeze(0)
+    d2 = planes_next(2, c2)
     f1 = planes_near(1, e1)
+    e0 = planes_far(0)
     arrive(d1)
     squeeze(1)
     squeeze(2)
@@ -329,7 +343,6 @@
     squeeze(3)
     extra = jnp.concatenate(extra, axis=1)
     bias_row, weight_row = extra[0:1], extra[1:2]
-    f0 = planes_near(0, e0)
 
     part32[...] = jnp.dot(cv[...], wc[...], preferred_element_type=F32)
     cross = jnp.sum(cot32[...] * part32[...], axis=1, keepdims=True)
@@ -338,18 +351,28 @@
     st[0:T, :] = jnp.where(lane == 0, plain, jnp.where(lane == 1, cross, 0.0))
     stats2[me] = st[...].T[0:2, :]
     ex2 = start([remote(stats2.at[me], stats2.at[me], to_intra(d)) for d in range(1, NI)])
-    h2 = rows_near(2, g2)
-    for s in range(NI):
-        pown[s] = pack(part32[OWN * s:OWN * s + OWN, :] + bias_row).astype(BF16)
-    exp = start([remote(pown.at[(me + d) % NI], pland.at[d - 1], to_intra(d)) for d in range(1, NI)])
-
-    planes_sum(1, f1)
-    g1 = rows_far(1)
-    rows_sum(2, h2)
+    def partial_rows(zl, c):
+        base = pl.multiple_of(OWN * (2 * zl + c), 8)
+        return pack(part32[pl.ds(base, OWN), :] + bias_row)
+
+    for zl in range(4):
+        pown[zl] = partial_rows(zl, 1 - core).astype(BF16)
+    pair = start([remote(pown, pmate, mate)])
+    f0 = planes_near(0, e0)
+    rows_sum(2, g2)
     rz1 = start([
         remote(scat3.at[0, 3], land5.at[0], to_grp("z", 1)),
         remote(scat3.at[1, 3], land5.at[1], to_grp("z", 3)),
     ])
+    arrive(pair)
+    for zl in range(4):
+        psum[zl] = (partial_rows(zl, core) + pmate[zl].astype(F32)).astype(BF16)
+    exp = start([
+        remote(psum.at[((me + d) % NI) // 2], pland.at[d // 2 - 1], to_intra(d)) for d in (2, 6, 4)
+    ])
+
+    planes_sum(1, f1)
+    g1 = rows_far(1)
 
     arrive(ex2)
     means = jnp.sum(stats2[...], axis=0) / D
@@ -368,33 +391,29 @@
         input_part(f)
     planes_sum(0, f0)
     g0 = rows_far(0)
-    h1 = rows_near(1, g1)
     for f in range(1024, F, 256):
         input_part(f)
     ig_copy = pltpu.make_async_copy(igv, ig_hbm, local.at[0])
     ig_copy.start()
 
-    h0 = rows_near(0, g0)
-    rows_sum(1, h1)
+    drain(len(started) - 24)
+    rows_sum(1, g1)
     arrive(rz1)
     scat3[0, 2] = (scat3[0, 2].astype(F32) + land5[0].astype(F32)).astype(BF16)
     scat3[1, 1] = (scat3[1, 1].astype(F32) + land5[1].astype(F32)).astype(BF16)
-    rz2 = start([
-        remote(scat3.at[:, 2], land6.at[0], to_grp("z", 1)),
-        remote(scat3.at[:, 1], land6.at[1], to_grp("z", 3)),
-    ])
+    rz2 = scatter_to(1, 3) + scatter_to(2, 1)
 
     arrive(exp)
-    total = pown[me].astype(F32)
-    for d in range(NI - 1):
+    total = psum[me // 2].astype(F32)
+    for d in range(3):
         total = total + pland[d].astype(F32)
     proj_ref[...] = unpack(total).astype(BF16)
 
-    mine = [part_sum(row_part, land4, "yx", 0, h0, h)[0] for h in (0, 1)]
+    mine = [part_sum(row_part, land4, "yx", 0, g0, h)[0] for h in (0, 1)]
     arrive(rz2)
-    total = jnp.concatenate([
-        mine[h] + land6[0, h].astype(F32) + land6[1, h].astype(F32) for h in (0, 1)
-    ], axis=1)
+    for k in range(2):
+        mine = [mine[h] + land6[k, h].astype(F32) for h in (0, 1)]
+    total = jnp.concatenate(mine, axis=1)
     sum_row = total[R:R + 1]
     weight = wfull[...]
     wg_ref[...] = (total * gain + bias * sum_row)[:R]
@@ -405,8 +424,7 @@
     gg_ref[...] = as_row(jnp.sum(weight * total, axis=1, keepdims=True))
     bg_ref[...] = as_row(jnp.sum(weight * sum_row, axis=1, keepdims=True))
 
-    for c in started:
-        c.wait_send()
+    drain(len(started))
     ig_copy.wait()
 
 
@@ -453,12 +471,12 @@
             v32(T, C), v16(T, C), v16(NI, 16, 1280), v32(F, C),
             v16(F, C), v32(T, C),
             v16(2, 4, 4, 4, SLOT, H), v16(2, 4, 4, 4, SLOT, H),
-            v16(2, 2, 4, 2, SLOT, H), v16(2, 2, 4, 4, SLOT, H),
-            v16(2, 4, 4, SLOT, H), v16(2, 2, 4, 16, H), v16(2, 2, 4, SLOT, H),
+            v16(2, 2, 4, 2, SLOT, H), v16(2, 3, 4, 4, SLOT, H),
+            v16(2, 4, 4, SLOT, H), v16(2, 3, 4, SLOT, H),
             v16(2, 4, SLOT, H), v16(2, SLOT, H), v16(2, 2, SLOT, H),
             v32(384, 128), v32(NI, 2, 384), v32(NI, 2, 384),
             v32(384, 128), v32(384, 128),
-            v16(NI, 16, 1280), v16(NI - 1, 16, 1280),
+            v16(4, 16, 1280), v16(4, 16, 1280), v16(4, 16, 1280), v16(3, 16, 1280),
             pltpu.SemaphoreType.DMA((COPIES,)),
             pltpu.SemaphoreType.DMA((COPIES,)),
             pltpu.SemaphoreType.DMA((5,)),

time: 68.1 us -> 61.5 us (0.903)
  Pallas kernels: 67.3 us -> 60.4 us
    pallas_call x1, Pallas kernels: 65.2 us -> 58.2 us  [shards(): pl.pallas_call(kernel, out_shape=shapes, in_specs=[hbm] * 5, out_specs=(v...]
where the time goes in v3:
time: 61.5 us; the launch traced here: 61 us
  Pallas kernels  60.4 us (98%)
  between operations  0.64 us (1%)
    pallas_call x1, Pallas kernels, shards(): pl.pallas_call(kernel, out_shape=shapes, in_specs=[hbm] * 5, out_specs=(v...  58.2 us
    pallas_call x1, Pallas kernels, shards(): pl.pallas_call(writer, out_shape=shapes, in_specs=[anywhere] * 5, out_spe...  2.16 us

profile of v3, /device:TPU:32, one launch (start us, length us, event | category | flops | bytes accessed | tf_op | source)
XLA Modules:
  0.0 61.0 jit_solution(16468424352700447201)
XLA Ops:
  0.6 58.2 %shard_map.92 = (bf16[40,512]{1,0:T(8,128)(2,1)}, bf16[320,1856]{1,0:T(8,128)(2,1)}, f32[29,512]{1,0:T(8,128)}, f32[1,29]{1,0:T(1,128)}, f32[1,29]{1,0:T(1,128)}) custom-call(bf16[320,1856]{1,0:T(8,128)(2,1)} %x_hbm.1, bf16[29,512]{1,0:T(8,128)(2,1)} %w_hbm.1, bf16[1,29]{1,0:T(2,128)(2,1)} %bitcast.4, bf16[1,29]{1,0:T(2,128)(2,1)} %bitcast.5, ...), custom_call_target="tpu_custom_call" | custom-call | tf_op jit(solution)/shard_map/pallas_call | solution.py:462
  58.9 2.2 %shard_map.93 = (bf16[40,512]{1,0:T(8,128)(2,1)}, bf16[320,1856]{1,0:T(8,128)(2,1)}, f32[29,512]{1,0:T(8,128)}, f32[1,29]{1,0:T(1,128)}, f32[1,29]{1,0:T(1,128)}) custom-call(bf16[40,512]{1,0:T(8,128)(2,1)} %get-tuple-element.15.a, bf16[320,1856]{1,0:T(8,128)(2,1)} %get-tuple-element.16.b, f32[29,512]{1,0:T(8,128)} %get-tuple-element.17.c, ...), custom_call_target="tpu_custom_call" | custom-call | tf_op jit(solution)/shard_map/pallas_call | solution.py:489

commit v4 on v3

--- a/solution.py
+++ b/solution.py
@@ -19,7 +19,7 @@
 NI = 8
 D = F * NI
 COPIES = 140
-GATHER_DIRECT = (False, False, True)
+GATHER_DIRECT = (False, False, False)
 SCATTER_DIRECT = (False, False, False)
 
 

time: 61.5 us -> 61.1 us (level)
  no operation moved by 1% of the time
where the time goes in v4:
time: 61.1 us; the launch traced here: 60.8 us
  Pallas kernels  60.1 us (98%)
  between operations  0.64 us (1%)
    pallas_call x1, Pallas kernels, shards(): pl.pallas_call(kernel, out_shape=shapes, in_specs=[hbm] * 5, out_specs=(v...  58 us
    pallas_call x1, Pallas kernels, shards(): pl.pallas_call(writer, out_shape=shapes, in_specs=[anywhere] * 5, out_spe...  2.16 us

profile of v4, /device:TPU:32, one launch (start us, length us, event | category | flops | bytes accessed | tf_op | source)
XLA Modules:
  0.0 60.8 jit_solution(9643304505463476852)
XLA Ops:
  0.6 58.0 %shard_map.92 = (bf16[40,512]{1,0:T(8,128)(2,1)}, bf16[320,1856]{1,0:T(8,128)(2,1)}, f32[29,512]{1,0:T(8,128)}, f32[1,29]{1,0:T(1,128)}, f32[1,29]{1,0:T(1,128)}) custom-call(bf16[320,1856]{1,0:T(8,128)(2,1)} %x_hbm.1, bf16[29,512]{1,0:T(8,128)(2,1)} %w_hbm.1, bf16[1,29]{1,0:T(2,128)(2,1)} %bitcast.4, bf16[1,29]{1,0:T(2,128)(2,1)} %bitcast.5, ...), custom_call_target="tpu_custom_call" | custom-call | tf_op jit(solution)/shard_map/pallas_call | solution.py:462
  58.6 2.2 %shard_map.93 = (bf16[40,512]{1,0:T(8,128)(2,1)}, bf16[320,1856]{1,0:T(8,128)(2,1)}, f32[29,512]{1,0:T(8,128)}, f32[1,29]{1,0:T(1,128)}, f32[1,29]{1,0:T(1,128)}) custom-call(bf16[40,512]{1,0:T(8,128)(2,1)} %get-tuple-element.15.a, bf16[320,1856]{1,0:T(8,128)(2,1)} %get-tuple-element.16.b, f32[29,512]{1,0:T(8,128)} %get-tuple-element.17.c, ...), custom_call_target="tpu_custom_call" | custom-call | tf_op jit(solution)/shard_map/pallas_call | solution.py:489

commit v5 on v4

--- a/solution.py
+++ b/solution.py
@@ -18,9 +18,9 @@
 OWN = 40
 NI = 8
 D = F * NI
-COPIES = 140
-GATHER_DIRECT = (False, False, False)
-SCATTER_DIRECT = (False, False, False)
+COPIES = 160
+GATHER_DIRECT = (False, False, False, False)
+SCATTER_DIRECT = (False, False, False, False)
 
 
 def pack(v):
@@ -106,7 +106,7 @@
         pl.semaphore_signal(barrier, inc=1, device_id=peer, device_id_type=MESH)
 
     plane_of = (z, up(z, 3), up(z, 1), up(z, 2))
-    groups = (slice(0, 1), slice(1, 3), slice(3, 4))
+    groups = tuple(slice(k, k + 1) for k in range(4))
 
     for load in loads[:3]:
         load.wait()
@@ -208,19 +208,21 @@
         v = xv[r:r + 64, :].astype(F32)
         cv[r:r + 64, :] = ((v - cols[r:r + 64, 0:1]) * cols[r:r + 64, 1:2]).astype(BF16)
 
-    arrive(gz1)
-    gz2 = start([
-        remote(gath.at[0, 1, y, x], gath.at[0, 3, y, x], to_grp("z", 1)),
-        remote(gath.at[1, 2, y, x], gath.at[1, 3, y, x], to_grp("z", 3)),
-    ])
+    arrive(gz1[:1])
+    gz2 = start([remote(gath.at[0, 1, y, x], gath.at[0, 3, y, x], to_grp("z", 1))])
     a1 = rows_own(1)
+    arrive(gz1[1:])
+    gz2 += start([remote(gath.at[1, 2, y, x], gath.at[1, 3, y, x], to_grp("z", 3))])
+    a2 = rows_own(2)
     d0 = planes_next(0, c0)
     arrive(a1)
     c1 = planes_own(1)
+    arrive(a2)
+    c2 = planes_own(2)
     arrive(ct1)
     ct2 = start([remote(cotg.at[(me + d) % NI], cotg.at[(me + d) % NI], mate) for d in (6, 2, 4)])
     arrive(gz2)
-    a2 = rows_own(2)
+    a3 = rows_own(3)
     arrive(ct0)
     arrive(ct2)
     for s in range(NI):
@@ -306,15 +308,17 @@
         return start([remote(scat3.at[:, slot], land6.at[slot - 1], to_grp("z", by))])
 
     spread(3)
-    e2 = planes_far(2)
-    arrive(a2)
-    c2 = planes_own(2)
+    e3 = planes_far(3)
+    arrive(a3)
+    c3 = planes_own(3)
     spread(1)
-    spread(2)
     e1 = planes_far(1)
     d1 = planes_next(1, c1)
+    spread(2)
+    e2 = planes_far(2)
+    d2 = planes_next(2, c2)
     spread(0)
-    f2 = planes_near(2, e2)
+    f3 = planes_near(3, e3)
     drain(30)
 
     extra = [jnp.zeros((8, H), F32), jnp.zeros((8, H), F32)]
@@ -331,15 +335,17 @@
 
     arrive(d0)
     squeeze(0)
-    d2 = planes_next(2, c2)
+    d3 = planes_next(3, c3)
     f1 = planes_near(1, e1)
+    f2 = planes_near(2, e2)
     e0 = planes_far(0)
     arrive(d1)
     squeeze(1)
+    arrive(d2)
     squeeze(2)
-    planes_sum(2, f2)
-    g2 = rows_far(2)
-    arrive(d2)
+    planes_sum(3, f3)
+    g3 = rows_far(3)
+    arrive(d3)
     squeeze(3)
     extra = jnp.concatenate(extra, axis=1)
     bias_row, weight_row = extra[0:1], extra[1:2]
@@ -359,7 +365,7 @@
         pown[zl] = partial_rows(zl, 1 - core).astype(BF16)
     pair = start([remote(pown, pmate, mate)])
     f0 = planes_near(0, e0)
-    rows_sum(2, g2)
+    rows_sum(3, g3)
     rz1 = start([
         remote(scat3.at[0, 3], land5.at[0], to_grp("z", 1)),
         remote(scat3.at[1, 3], land5.at[1], to_grp("z", 3)),
@@ -373,6 +379,8 @@
 
     planes_sum(1, f1)
     g1 = rows_far(1)
+    planes_sum(2, f2)
+    g2 = rows_far(2)
 
     arrive(ex2)
     means = jnp.sum(stats2[...], axis=0) / D
@@ -399,9 +407,11 @@
     drain(len(started) - 24)
     rows_sum(1, g1)
     arrive(rz1)
+    scat3[1, 1] = (scat3[1, 1].astype(F32) + land5[1].astype(F32)).astype(BF16)
+    rz2 = scatter_to(1, 3)
+    rows_sum(2, g2)
     scat3[0, 2] = (scat3[0, 2].astype(F32) + land5[0].astype(F32)).astype(BF16)
-    scat3[1, 1] = (scat3[1, 1].astype(F32) + land5[1].astype(F32)).astype(BF16)
-    rz2 = scatter_to(1, 3) + scatter_to(2, 1)
+    rz2 += scatter_to(2, 1)
 
     arrive(exp)
     total = psum[me // 2].astype(F32)

time: 61.1 us -> 62 us (1.015)
  Pallas kernels: 60.1 us -> 61.2 us
    pallas_call x1, Pallas kernels: 58 us -> 59 us  [shards(): pl.pallas_call(kernel, out_shape=shapes, in_specs=[hbm] * 5, out_specs=(v...]
where the time goes in v5:
time: 62 us; the launch traced here: 61.8 us
  Pallas kernels  61.2 us (99%)
  between operations  0.64 us (1%)
    pallas_call x1, Pallas kernels, shards(): pl.pallas_call(kernel, out_shape=shapes, in_specs=[hbm] * 5, out_specs=(v...  59 us
    pallas_call x1, Pallas kernels, shards(): pl.pallas_call(writer, out_shape=shapes, in_specs=[anywhere] * 5, out_spe...  2.16 us

profile of v5, /device:TPU:32, one launch (start us, length us, event | category | flops | bytes accessed | tf_op | source)
XLA Modules:
  0.0 61.8 jit_solution(12815278186336767438)
XLA Ops:
  0.6 59.0 %shard_map.92 = (bf16[40,512]{1,0:T(8,128)(2,1)}, bf16[320,1856]{1,0:T(8,128)(2,1)}, f32[29,512]{1,0:T(8,128)}, f32[1,29]{1,0:T(1,128)}, f32[1,29]{1,0:T(1,128)}) custom-call(bf16[320,1856]{1,0:T(8,128)(2,1)} %x_hbm.1, bf16[29,512]{1,0:T(8,128)(2,1)} %w_hbm.1, bf16[1,29]{1,0:T(2,128)(2,1)} %bitcast.4, bf16[1,29]{1,0:T(2,128)(2,1)} %bitcast.5, ...), custom_call_target="tpu_custom_call" | custom-call | tf_op jit(solution)/shard_map/pallas_call | solution.py:472
  59.6 2.2 %shard_map.93 = (bf16[40,512]{1,0:T(8,128)(2,1)}, bf16[320,1856]{1,0:T(8,128)(2,1)}, f32[29,512]{1,0:T(8,128)}, f32[1,29]{1,0:T(1,128)}, f32[1,29]{1,0:T(1,128)}) custom-call(bf16[40,512]{1,0:T(8,128)(2,1)} %get-tuple-element.15.a, bf16[320,1856]{1,0:T(8,128)(2,1)} %get-tuple-element.16.b, f32[29,512]{1,0:T(8,128)} %get-tuple-element.17.c, ...), custom_call_target="tpu_custom_call" | custom-call | tf_op jit(solution)/shard_map/pallas_call | solution.py:499
